TPU v7x, 32 devices: a whole 2x2x4 slice. The times are simulated.
32 devices in a mesh: groups: 2 (over y), seq: 16 (over z, x, core).
Axes of the slice: x: 2, y: 2, z: 4, core: 2. Of those that a mesh axis runs over, the one named last changes fastest.
Arguments:
- queries: bfloat16 [4, 128, 128, 128], P('groups', 'seq'), parts along dimension 0, may hold values from -64 to 64
- new_k: bfloat16 [4, 128, 8, 128], P('groups', 'seq'), parts along dimension 0, may hold values from -15 to 15
- new_v: bfloat16 [4, 128, 8, 128], P('groups', 'seq'), parts along dimension 0, may hold values from -6 to 6
- cache_k: bfloat16 [4, 8192, 8, 128], P('groups', 'seq'), parts along dimension 0, may hold values from -12 to 12
- cache_v: bfloat16 [4, 8192, 8, 128], P('groups', 'seq'), parts along dimension 0, may hold values from -6 to 6
- cache_len: int32 [4], P('groups'), parts along dimension 0, may hold values from 2048 to 8192
Outputs:
- attended: bfloat16 [4, 128, 128, 128], P('groups', 'seq'), parts along dimension 0
There are 2 independent parts, one for each index of `groups`. A program takes and returns all parts, laid end to end along the dimension named above; each array names one. Nothing has to cross between parts.
Inputs may be any that keep to these rules, and one draw needn't show every extreme that they name: The first cache_len[r] of the 8192 cache slots of request r hold keys and values; the rest are to be ignored.
All inputs are finite; a program needn't handle non-finite values.
Results may differ from a plain program's by a relative error of at most 0.004.
Values may be sent and summed in bfloat16 or wider, within the bound.
A program may use at most 128 MiB of HBM per device.

v0:
```python
import math

import jax
import jax.numpy as jnp
from jax import lax
from jax.sharding import PartitionSpec as P


def shards(queries, new_k, new_v, cache_k, cache_v, cache_len):
    requests, local_rows, heads, head_dim = queries.shape
    slots = cache_k.shape[1]
    kv_heads = cache_k.shape[2]
    group_size = heads // kv_heads
    devices_seq = lax.axis_size("seq")
    seq_index = lax.axis_index("seq")
    scaling = 1.0 / math.sqrt(head_dim)
    all_rows = local_rows * devices_seq
    spread = devices_seq // kv_heads
    piece = slots // spread
    part_id = seq_index % spread

    def to_heads(cache):
        moved = cache.reshape(requests, spread, piece, kv_heads, head_dim)
        return jnp.transpose(moved, (3, 1, 0, 2, 4)).reshape(devices_seq, requests, piece, head_dim)

    moved_k, moved_v = (
        lax.all_to_all(to_heads(cache_k), "seq", split_axis=0, concat_axis=0, tiled=True),
        lax.all_to_all(to_heads(cache_v), "seq", split_axis=0, concat_axis=0, tiled=True),
    )
    grouped = jnp.transpose(
        queries.reshape(requests, local_rows, kv_heads, group_size, head_dim), (2, 1, 0, 3, 4)
    )
    grouped = jnp.broadcast_to(
        grouped[:, None], (kv_heads, spread, local_rows, requests, group_size, head_dim)
    )
    grouped = grouped.reshape(devices_seq, local_rows, requests, group_size, head_dim)

    def head_spread(fresh):
        turned = jnp.transpose(fresh, (2, 1, 0, 3))
        turned = jnp.broadcast_to(
            turned[:, None], (kv_heads, spread, local_rows, requests, head_dim)
        )
        return turned.reshape(devices_seq, local_rows, requests, head_dim)

    head_q, head_k, head_v = (
        lax.all_to_all(grouped, "seq", split_axis=0, concat_axis=1, tiled=True),
        lax.all_to_all(head_spread(new_k), "seq", split_axis=0, concat_axis=1, tiled=True),
        lax.all_to_all(head_spread(new_v), "seq", split_axis=0, concat_axis=1, tiled=True),
    )
    head_q = head_q[0]
    head_k = head_k[0]
    head_v = head_v[0]
    slot_pos = (
        jnp.arange(devices_seq, dtype=jnp.int32)[:, None] * slots
        + part_id * piece
        + jnp.arange(piece, dtype=jnp.int32)[None, :]
    ).reshape(-1)
    head_valid = (slot_pos[None, :] < cache_len[:, None])[:, None, None, :]
    fresh_pos = jnp.arange(all_rows, dtype=jnp.int32)
    held_slots = devices_seq * piece
    block_rows = max((width for width in range(1, min(all_rows, 16) + 1) if all_rows % width == 0))

    def head_block(block, state):
        start = block * block_rows
        sub_rows = lax.dynamic_slice_in_dim(head_q, start, block_rows, 0)
        cache_scores = jnp.einsum(
            "prgd,srjd->rpgsj", sub_rows, moved_k, preferred_element_type=jnp.float32
        )
        cache_scores = cache_scores.reshape(requests, block_rows, group_size, held_slots) * scaling
        fresh_scores = (
            jnp.einsum("prgd,urd->rpgu", sub_rows, head_k, preferred_element_type=jnp.float32)
            * scaling
        )
        row_pos = start + jnp.arange(block_rows, dtype=jnp.int32)
        fresh_valid = ((fresh_pos[None, :] <= row_pos[:, None]) & (part_id == 0))[None, :, None, :]
        cache_scores = jnp.where(head_valid, cache_scores, -1e30)
        fresh_scores = jnp.where(fresh_valid, fresh_scores, -1e30)
        row_max = jnp.maximum(jnp.max(cache_scores, axis=-1), jnp.max(fresh_scores, axis=-1))
        cache_weights = jnp.where(head_valid, jnp.exp(cache_scores - row_max[..., None]), 0.0)
        fresh_weights = jnp.where(fresh_valid, jnp.exp(fresh_scores - row_max[..., None]), 0.0)
        row_sum = jnp.sum(cache_weights, axis=-1) + jnp.sum(fresh_weights, axis=-1)
        cache_weights = cache_weights.astype(jnp.bfloat16).reshape(
            requests, block_rows, group_size, devices_seq, piece
        )
        partial_value = jnp.einsum(
            "rpgsj,srjd->prgd", cache_weights, moved_v, preferred_element_type=jnp.float32
        )
        partial_value = partial_value + jnp.einsum(
            "rpgu,urd->prgd",
            fresh_weights.astype(jnp.bfloat16),
            head_v,
            preferred_element_type=jnp.float32,
        )
        results = (
            partial_value,
            jnp.transpose(row_max, (1, 0, 2)),
            jnp.transpose(row_sum, (1, 0, 2)),
        )
        return tuple(
            (
                lax.dynamic_update_slice_in_dim(whole, piece_out, start, 0)
                for whole, piece_out in zip(state, results)
            )
        )

    start_state = (
        jnp.zeros((all_rows, requests, group_size, head_dim), jnp.float32),
        jnp.full((all_rows, requests, group_size), -1e30, jnp.float32),
        jnp.zeros((all_rows, requests, group_size), jnp.float32),
    )
    partial_value, row_max, row_sum = lax.fori_loop(
        0, all_rows // block_rows, head_block, start_state
    )
    partial_value = partial_value.reshape(devices_seq, local_rows, requests, group_size, head_dim)
    row_max = row_max.reshape(devices_seq, local_rows, requests, group_size)
    row_sum = row_sum.reshape(devices_seq, local_rows, requests, group_size)
    partial_value, row_max, row_sum = (
        lax.all_to_all(partial_value, "seq", split_axis=0, concat_axis=0, tiled=True),
        lax.all_to_all(row_max, "seq", split_axis=0, concat_axis=0, tiled=True),
        lax.all_to_all(row_sum, "seq", split_axis=0, concat_axis=0, tiled=True),
    )
    partial_value = partial_value.reshape(
        kv_heads, spread, local_rows, requests, group_size, head_dim
    )
    row_max = row_max.reshape(kv_heads, spread, local_rows, requests, group_size)
    row_sum = row_sum.reshape(kv_heads, spread, local_rows, requests, group_size)
    global_max = jnp.max(row_max, axis=1)
    rescale = jnp.exp(row_max - global_max[:, None])
    numerator = jnp.sum(partial_value * rescale[..., None], axis=1)
    denominator = jnp.sum(row_sum * rescale, axis=1)
    merged = numerator / denominator[..., None]
    merged = jnp.transpose(merged, (2, 1, 0, 3, 4)).reshape(requests, local_rows, heads, head_dim)
    return merged.astype(jnp.bfloat16)


def solution(mesh):
    in_specs = (
        P("groups", "seq", None, None),
        P("groups", "seq", None, None),
        P("groups", "seq", None, None),
        P("groups", "seq", None, None),
        P("groups", "seq", None, None),
        P("groups"),
    )
    out_specs = P("groups", "seq", None, None)
    return jax.shard_map(shards, mesh=mesh, in_specs=in_specs, out_specs=out_specs, check_vma=False)
```

profile of v0, /device:TPU:9, one launch (start us, length us, event | category | flops | bytes accessed | tf_op | source)
XLA Modules:
  0.0 310.1 jit_solution(9602894458382184402)
XLA Ops:
  1.4 6.6 %all-to-all-start.4 = ((bf16[16,8,2,128]{3,1,2,0:T(8,128)(2,1)}), bf16[16,8,2,128]{3,1,2,0:T(8,128)(2,1)S(1)}, u32[]{:S(2)}, u32[]{:S(2)}) async-start(bf16[16,8,2,128]{3,1,2,0:T(8,128)(2,1)} %bitcast.14), calls=%async_computation.4 | async-start | bytes 131072 | tf_op jit(solution)/shard_map/all_to_all | solution.py:48
  8.8 4.3 %all-to-all-done.4 = bf16[16,8,2,128]{3,1,2,0:T(8,128)(2,1)S(1)} async-done(((bf16[16,8,2,128]{3,1,2,0:T(8,128)(2,1)}), bf16[16,8,2,128]{3,1,2,0:T(8,128)(2,1)S(1)}, u32[]{:S(2)}, u32[]{:S(2)}) %all-to-all-start.4) | async-done | bytes 65568 | tf_op jit(solution)/shard_map/all_to_all | solution.py:48
  13.7 5.2 %all-to-all-start.2 = ((bf16[16,8,2,128]{3,1,2,0:T(8,128)(2,1)}), bf16[16,8,2,128]{3,1,2,0:T(8,128)(2,1)S(1)}, u32[]{:S(2)}, u32[]{:S(2)}) async-start(bf16[16,8,2,128]{3,1,2,0:T(8,128)(2,1)} %bitcast.8), calls=%async_computation.2 | async-start | bytes 131072 | tf_op jit(solution)/shard_map/all_to_all | solution.py:47
  20.0 4.0 %all-to-all-done.2 = bf16[16,8,2,128]{3,1,2,0:T(8,128)(2,1)S(1)} async-done(((bf16[16,8,2,128]{3,1,2,0:T(8,128)(2,1)}), bf16[16,8,2,128]{3,1,2,0:T(8,128)(2,1)S(1)}, u32[]{:S(2)}, u32[]{:S(2)}) %all-to-all-start.2) | async-done | bytes 65568 | tf_op jit(solution)/shard_map/all_to_all | solution.py:47
  25.3 5.4 %all-to-all-start = ((bf16[16,8,2,16,128]{4,3,1,2,0:T(8,128)(2,1)}), bf16[16,8,2,16,128]{4,3,1,2,0:T(8,128)(2,1)S(1)}, u32[]{:S(2)}, u32[]{:S(2)}) async-start(bf16[16,8,2,16,128]{4,3,1,2,0:T(8,128)(2,1)} %bitcast.2), calls=%async_computation | async-start | bytes 2097152 | tf_op jit(solution)/shard_map/all_to_all | solution.py:46
  30.7 3.4 %copy.52 = bf16[2,2,256,8,128]{4,2,0,1,3:T(8,128)(2,1)} copy(bf16[2,2,256,8,128]{4,3,2,1,0:T(8,128)(2,1)} %bitcast.129) | data formatting | bytes 4194304 | tf_op jit(solution)/shard_map/reshape | solution.py:23
  34.0 21.5 %all-to-all-done = bf16[16,8,2,16,128]{4,3,1,2,0:T(8,128)(2,1)S(1)} async-done(((bf16[16,8,2,16,128]{4,3,1,2,0:T(8,128)(2,1)}), bf16[16,8,2,16,128]{4,3,1,2,0:T(8,128)(2,1)S(1)}, u32[]{:S(2)}, u32[]{:S(2)}) %all-to-all-start) | async-done | bytes 1048608 | tf_op jit(solution)/shard_map/all_to_all | solution.py:46
  55.6 4.9 %all-to-all-start.1 = ((bf16[16,2,256,128]{3,2,1,0:T(8,128)(2,1)}), bf16[16,2,256,128]{3,2,1,0:T(8,128)(2,1)S(1)}, u32[]{:S(2)}, u32[]{:S(2)}) async-start(bf16[16,2,256,128]{3,2,1,0:T(8,128)(2,1)} %bitcast.125), calls=%async_computation.1 | async-start | bytes 4194304 | tf_op jit(solution)/shard_map/all_to_all | solution.py:27
  60.5 3.4 %copy.55 = bf16[2,2,256,8,128]{4,2,0,1,3:T(8,128)(2,1)} copy(bf16[2,2,256,8,128]{4,3,2,1,0:T(8,128)(2,1)} %bitcast.130) | data formatting | bytes 4194304 | tf_op jit(solution)/shard_map/reshape | solution.py:23
  63.9 42.6 %all-to-all-done.1 = bf16[16,2,256,128]{3,2,1,0:T(8,128)(2,1)S(1)} async-done(((bf16[16,2,256,128]{3,2,1,0:T(8,128)(2,1)}), bf16[16,2,256,128]{3,2,1,0:T(8,128)(2,1)S(1)}, u32[]{:S(2)}, u32[]{:S(2)}) %all-to-all-start.1) | async-done | bytes 2097184 | tf_op jit(solution)/shard_map/all_to_all | solution.py:27
  106.5 1.3 copy-done
  107.8 6.3 %all-to-all-start.3 = ((bf16[16,2,256,128]{3,2,1,0:T(8,128)(2,1)}), bf16[16,2,256,128]{3,2,1,0:T(8,128)(2,1)}, u32[]{:S(2)}, u32[]{:S(2)}) async-start(bf16[16,2,256,128]{3,2,1,0:T(8,128)(2,1)} %bitcast.122), calls=%async_computation.3 | async-start | bytes 4194304 | tf_op jit(solution)/shard_map/all_to_all | solution.py:28
  114.5 1.2 copy-done.1
  115.9 44.3 %all-to-all-done.3 = bf16[16,2,256,128]{3,2,1,0:T(8,128)(2,1)} async-done(((bf16[16,2,256,128]{3,2,1,0:T(8,128)(2,1)}), bf16[16,2,256,128]{3,2,1,0:T(8,128)(2,1)}, u32[]{:S(2)}, u32[]{:S(2)}) %all-to-all-start.3) | async-done | bytes 2097184 | tf_op jit(solution)/shard_map/all_to_all | solution.py:28
  160.2 3.2 %copy.60 = bf16[16,2,256,128]{3,2,0,1:T(8,128)(2,1)} copy(bf16[16,2,256,128]{3,2,1,0:T(8,128)(2,1)} %all-to-all-done.3) | data formatting | bytes 4194304
  163.4 1.4 broadcast_in_dim.120
  164.9 70.1 %while.20 = (s32[]{:T(128)}, f32[128,2,16,128]{3,2,0,1:T(8,128)}, f32[128,2,16]{2,0,1:T(8,128)S(1)}, f32[128,2,16]{2,0,1:T(8,128)S(1)}, bf16[128,2,16,128]{3,2,1...) while((s32[]{:T(128)}, f32[128,2,16,128]{3,2,0,1:T(8,128)}, ...), condition=%wide.region_5.6_spmd.clone, body=%wide.region_0.5_spmd.clone.sunk | while | flops 1135225856 | bytes 39920000 | solution.py:111
  166.0 1.4 fusion.61
  167.5 2.5 fusion.66
  170.3 2.4 fusion.64
  174.8 1.4 fusion.61
  176.3 2.5 fusion.66
  179.0 2.4 fusion.64
  183.6 1.4 fusion.61
  185.0 2.5 fusion.66
  187.8 2.4 fusion.64
  192.3 1.4 fusion.61
  193.8 2.5 fusion.66
  196.5 2.4 fusion.64
  201.1 1.4 fusion.61
  202.5 2.5 fusion.66
  205.3 2.4 fusion.64
  209.8 1.4 fusion.61
  211.3 2.5 fusion.66
  214.0 2.4 fusion.64
  218.6 1.4 fusion.61
  220.1 2.5 fusion.66
  222.8 2.4 fusion.64
  227.3 1.4 fusion.61
  228.8 2.5 fusion.66
  231.5 2.4 fusion.64
  235.7 6.3 %all-to-all-start.6 = ((f32[16,1,256]{2,1,0:T(1,128)}), f32[16,1,256]{2,1,0:T(1,128)S(1)}, u32[]{:S(2)}, u32[]{:S(2)}) async-start(f32[16,1,256]{2,1,0:T(1,128)} %reshape.224), calls=%async_computation.6 | async-start | bytes 32768 | tf_op jit(solution)/shard_map/all_to_all | solution.py:119
  242.7 4.3 %all-to-all-done.6 = f32[16,1,256]{2,1,0:T(1,128)S(1)} async-done(((f32[16,1,256]{2,1,0:T(1,128)}), f32[16,1,256]{2,1,0:T(1,128)S(1)}, u32[]{:S(2)}, u32[]{:S(2)}) %all-to-all-start.6) | async-done | bytes 16416 | tf_op jit(solution)/shard_map/all_to_all | solution.py:119
  247.0 4.9 %all-to-all-start.7 = ((f32[16,1,256]{2,1,0:T(1,128)}), f32[16,1,256]{2,1,0:T(1,128)S(1)}, u32[]{:S(2)}, u32[]{:S(2)}) async-start(f32[16,1,256]{2,1,0:T(1,128)} %reshape.226), calls=%async_computation.7 | async-start | bytes 32768 | tf_op jit(solution)/shard_map/all_to_all | solution.py:120
  251.9 3.2 %copy.62 = f32[16,8,2,16,128]{4,3,1,2,0:T(8,128)} copy(f32[16,8,2,16,128]{4,3,1,0,2:T(8,128)} %bitcast.124) | data formatting | bytes 4194304 | tf_op jit(solution)/shard_map/reshape | solution.py:114
  255.1 1.9 all-to-all-done.7
  257.0 5.1 %all-to-all-start.5 = ((f32[16,8,2,16,128]{4,3,1,2,0:T(8,128)}), f32[16,8,2,16,128]{4,3,1,2,0:T(8,128)S(1)}, u32[]{:S(2)}, u32[]{:S(2)}) async-start(f32[16,8,2,16,128]{4,3,1,2,0:T(8,128)} %copy.62), calls=%async_computation.5 | async-start | bytes 4194304 | tf_op jit(solution)/shard_map/all_to_all | solution.py:118
  264.2 43.9 %all-to-all-done.5 = f32[16,8,2,16,128]{4,3,1,2,0:T(8,128)S(1)} async-done(((f32[16,8,2,16,128]{4,3,1,2,0:T(8,128)}), f32[16,8,2,16,128]{4,3,1,2,0:T(8,128)S(1)}, u32[]{:S(2)}, u32[]{:S(2)}) %all-to-all-start.5) | async-done | bytes 2097184 | tf_op jit(solution)/shard_map/all_to_all | solution.py:118
  (119 shorter events, 30.1 us)
Async XLA Ops:
  1.4 11.6 %all-to-all-start.4 = ((bf16[16,8,2,128]{3,1,2,0:T(8,128)(2,1)}), bf16[16,8,2,128]{3,1,2,0:T(8,128)(2,1)S(1)}, u32[]{:S(2)}, u32[]{:S(2)}) async-start(bf16[16,8,2,128]{3,1,2,0:T(8,128)(2,1)} %bitcast.14), calls=%async_computation.4 | async-start | bytes 131072 | tf_op jit(solution)/shard_map/all_to_all | solution.py:48
  13.7 10.4 %all-to-all-start.2 = ((bf16[16,8,2,128]{3,1,2,0:T(8,128)(2,1)}), bf16[16,8,2,128]{3,1,2,0:T(8,128)(2,1)S(1)}, u32[]{:S(2)}, u32[]{:S(2)}) async-start(bf16[16,8,2,128]{3,1,2,0:T(8,128)(2,1)} %bitcast.8), calls=%async_computation.2 | async-start | bytes 131072 | tf_op jit(solution)/shard_map/all_to_all | solution.py:47
  25.3 30.3 %all-to-all-start = ((bf16[16,8,2,16,128]{4,3,1,2,0:T(8,128)(2,1)}), bf16[16,8,2,16,128]{4,3,1,2,0:T(8,128)(2,1)S(1)}, u32[]{:S(2)}, u32[]{:S(2)}) async-start(bf16[16,8,2,16,128]{4,3,1,2,0:T(8,128)(2,1)} %bitcast.2), calls=%async_computation | async-start | bytes 2097152 | tf_op jit(solution)/shard_map/all_to_all | solution.py:46
  55.6 50.9 %all-to-all-start.1 = ((bf16[16,2,256,128]{3,2,1,0:T(8,128)(2,1)}), bf16[16,2,256,128]{3,2,1,0:T(8,128)(2,1)S(1)}, u32[]{:S(2)}, u32[]{:S(2)}) async-start(bf16[16,2,256,128]{3,2,1,0:T(8,128)(2,1)} %bitcast.125), calls=%async_computation.1 | async-start | bytes 4194304 | tf_op jit(solution)/shard_map/all_to_all | solution.py:27
  106.5 1.3 copy-start
  107.8 52.4 %all-to-all-start.3 = ((bf16[16,2,256,128]{3,2,1,0:T(8,128)(2,1)}), bf16[16,2,256,128]{3,2,1,0:T(8,128)(2,1)}, u32[]{:S(2)}, u32[]{:S(2)}) async-start(bf16[16,2,256,128]{3,2,1,0:T(8,128)(2,1)} %bitcast.122), calls=%async_computation.3 | async-start | bytes 4194304 | tf_op jit(solution)/shard_map/all_to_all | solution.py:28
  114.2 1.6 copy-start.1
  167.5 2.7 copy-start.2
  176.3 2.7 copy-start.2
  185.0 2.7 copy-start.2
  193.8 2.7 copy-start.2
  202.5 2.7 copy-start.2
  211.3 2.7 copy-start.2
  220.0 2.7 copy-start.2
  228.8 2.7 copy-start.2
  235.7 11.3 %all-to-all-start.6 = ((f32[16,1,256]{2,1,0:T(1,128)}), f32[16,1,256]{2,1,0:T(1,128)S(1)}, u32[]{:S(2)}, u32[]{:S(2)}) async-start(f32[16,1,256]{2,1,0:T(1,128)} %reshape.224), calls=%async_computation.6 | async-start | bytes 32768 | tf_op jit(solution)/shard_map/all_to_all | solution.py:119
  247.0 10.0 %all-to-all-start.7 = ((f32[16,1,256]{2,1,0:T(1,128)}), f32[16,1,256]{2,1,0:T(1,128)S(1)}, u32[]{:S(2)}, u32[]{:S(2)}) async-start(f32[16,1,256]{2,1,0:T(1,128)} %reshape.226), calls=%async_computation.7 | async-start | bytes 32768 | tf_op jit(solution)/shard_map/all_to_all | solution.py:120
  257.0 51.1 %all-to-all-start.5 = ((f32[16,8,2,16,128]{4,3,1,2,0:T(8,128)}), f32[16,8,2,16,128]{4,3,1,2,0:T(8,128)S(1)}, u32[]{:S(2)}, u32[]{:S(2)}) async-start(f32[16,8,2,16,128]{4,3,1,2,0:T(8,128)} %copy.62), calls=%async_computation.5 | async-start | bytes 4194304 | tf_op jit(solution)/shard_map/all_to_all | solution.py:118
where the time goes:
time: 313 us; the launch traced here: 310 us
  waiting for transfers between devices  167 us (53%)
  starting transfers between devices  44.9 us (14%)
  matrix products  41 us (13%)
  other arithmetic  31 us (10%)
  local copies, waits for them, and re-layouts  25.7 us (8%)
    all_to_all x1, waiting for transfers between devices, shards(): lax.all_to_all(to_heads(cache_v), 'seq', split_axis=0, concat_axis=0, til...  44.3 us
    all_to_all x1, waiting for transfers between devices, shards(): lax.all_to_all(partial_value, 'seq', split_axis=0, concat_axis=0, tiled=T...  43.9 us
    all_to_all x1, waiting for transfers between devices, shards(): lax.all_to_all(to_heads(cache_k), 'seq', split_axis=0, concat_axis=0, til...  42.6 us
    reduce_sum x16, other arithmetic, head_block(): row_sum = jnp.sum(cache_weights, axis=-1) + jnp.sum(fresh_weights, axis=-1)  21.7 us
    all_to_all x1, waiting for transfers between devices, shards(): lax.all_to_all(grouped, 'seq', split_axis=0, concat_axis=1, tiled=True)  21.5 us
    dot_general x8, matrix products, head_block(): jnp.einsum('rpgsj,srjd->prgd', cache_weights, moved_v, preferred_element_...  19.3 us
    dot_general x8, matrix products, head_block(): jnp.einsum('prgd,srjd->rpgsj', sub_rows, moved_k, preferred_element_type=...  11.5 us
    dot_general x8, matrix products, head_block(): jnp.einsum('rpgu,urd->prgd', fresh_weights.astype(jnp.bfloat16), head_v,...  7.78 us
  transfers between devices with their start and end apart: 8, of which 8 were waited for; matrix products, arithmetic and copies ran while one was open for 5% of the time, Pallas kernels for 0%

commit v1 on v0

v1 whole, which is shorter than its diff:
```python
import functools
import math

import jax
import jax.numpy as jnp
from jax import lax
from jax.experimental import pallas as pl
from jax.experimental.pallas import tpu as pltpu
from jax.sharding import PartitionSpec as P

MESH = pl.DeviceIdType.MESH
LOW = -1e30


def loop(start, stop, body):
    def step(i, carry):
        body(i)
        return carry

    lax.fori_loop(start, stop, step, jnp.int32(0))


def kernel(
    n, heads, requests, slots, local_rows, group, owners, span,
    len_ref, q_ref, new_ref, k_ref, v_ref, out_ref,
    all_q, all_new, all_k, all_v, part, stat, got, got_stat,
    own_sem, q_send, q_recv, new_send, new_recv, k_send, k_recv, v_send, v_recv,
    o_send, o_recv, s_send, s_recv,
):
    me = lax.axis_index("seq")
    block = me // heads
    my_head = lax.rem(me, heads)
    base = block * heads
    blocks = n // heads
    rows = local_rows * group
    padded = all_new.shape[3]
    head_dim = q_ref.shape[-1]
    factor = math.log2(math.e) / math.sqrt(head_dim)

    barrier = pltpu.get_barrier_semaphore()
    loop(1, n, lambda i: pl.semaphore_signal(
        barrier, inc=1, device_id={"seq": lax.rem(me + i, n)}, device_id_type=MESH))
    pl.semaphore_wait(barrier, n - 1)

    def remote(src, dst, send, recv, device):
        return pltpu.make_async_remote_copy(
            src_ref=src, dst_ref=dst, send_sem=send, recv_sem=recv,
            device_id={"seq": device}, device_id_type=MESH)

    def q_copy(device, source):
        return remote(q_ref.at[lax.rem(device, heads)], all_q.at[:, source],
                      q_send.at[device], q_recv.at[source], device)

    def new_copy(j, source):
        return remote(new_ref.at[j], all_new.at[:, :, source],
                      new_send.at[j], new_recv.at[source], base + j)

    def k_copy(r, j, source):
        return remote(k_ref.at[j, r], all_k.at[r, source],
                      k_send.at[r, j], k_recv.at[r, source], base + j)

    def v_copy(r, j, source):
        return remote(v_ref.at[j, r], all_v.at[r, source],
                      v_send.at[r, j], v_recv.at[r, source], base + j)

    def o_copy(r, device, source):
        return remote(part.at[r, device], got.at[r, source],
                      o_send.at[r, device], o_recv.at[r, source], device)

    def s_copy(r, device, source):
        return remote(stat.at[r, device], got_stat.at[r, source],
                      s_send.at[r, device], s_recv.at[r, source], device)

    other = lambda i: lax.rem(me + i, n)
    peer = lambda i: lax.rem(my_head + i, heads)

    loop(1, n, lambda i: q_copy(other(i), me).start())
    loop(1, heads, lambda i: new_copy(peer(i), my_head).start())
    for r in range(requests):
        loop(1, heads, lambda i: k_copy(r, peer(i), my_head).start())
        loop(1, heads, lambda i: v_copy(r, peer(i), my_head).start())

    own = [
        pltpu.make_async_copy(q_ref.at[my_head], all_q.at[:, me], own_sem.at[0]),
        pltpu.make_async_copy(new_ref.at[my_head], all_new.at[:, :, my_head], own_sem.at[1]),
    ]
    for r in range(requests):
        own.append(pltpu.make_async_copy(
            k_ref.at[my_head, r], all_k.at[r, my_head], own_sem.at[2 + 2 * r]))
        own.append(pltpu.make_async_copy(
            v_ref.at[my_head, r], all_v.at[r, my_head], own_sem.at[3 + 2 * r]))
    for copy in own:
        copy.start()
    for copy in own:
        copy.wait()

    loop(1, n, lambda i: q_copy(me, other(i)).wait_recv())
    loop(1, heads, lambda i: new_copy(my_head, peer(i)).wait_recv())

    step_rows = owners * rows
    steps = n // owners
    for r in range(requests):
        loop(1, heads, lambda i: k_copy(r, my_head, peer(i)).wait_recv())
        loop(1, heads, lambda i: v_copy(r, my_head, peer(i)).wait_recv())
        filled = len_ref[r]

        def attend(i, r=r, filled=filled):
            step = lax.rem(i + me, steps)
            first = step * owners
            q = all_q[r, pl.ds(first, owners)].reshape(step_rows, head_dim)

            def absorb(state, scores, values):
                peak, total, value = state
                new_peak = jnp.maximum(peak, jnp.max(scores, axis=1, keepdims=True))
                rescale = jnp.exp2(peak - new_peak)
                weights = jnp.exp2(scores - new_peak)
                total = total * rescale + jnp.sum(weights, axis=1, keepdims=True)
                value = value * rescale + jnp.dot(
                    weights.astype(jnp.bfloat16), values, preferred_element_type=jnp.float32)
                return new_peak, total, value

            def score(keys):
                return lax.dot_general(
                    q, keys, (((1,), (1,)), ((), ())),
                    preferred_element_type=jnp.float32) * factor

            state = (
                jnp.full((step_rows, 1), LOW, jnp.float32),
                jnp.zeros((step_rows, 1), jnp.float32),
                jnp.zeros((step_rows, head_dim), jnp.float32),
            )
            for c in range(0, heads, span):
                keys = all_k[r, c:c + span].reshape(span * slots, head_dim)
                values = all_v[r, c:c + span].reshape(span * slots, head_dim)
                pos = (base + c) * slots + lax.broadcasted_iota(
                    jnp.int32, (1, span * slots), 1)
                bias = jnp.where(pos < filled, 0.0, LOW)
                state = absorb(state, score(keys) + bias, values)
            width = heads * padded
            keys = all_new[r, 0].reshape(width, head_dim)
            values = all_new[r, 1].reshape(width, head_dim)
            lane = lax.broadcasted_iota(jnp.int32, (step_rows, width), 1)
            row = lax.broadcasted_iota(jnp.int32, (step_rows, width), 0)
            inner = lax.rem(lane, padded)
            key_pos = (base + lax.div(lane, padded)) * local_rows + inner
            row_pos = first * local_rows + lax.div(row, group)
            valid = (inner < local_rows) & (key_pos <= row_pos)
            peak, total, value = absorb(
                state, jnp.where(valid, score(keys), LOW), values)

            result = (value / total).astype(jnp.bfloat16).reshape(owners, rows, head_dim)
            lanes = lax.broadcasted_iota(jnp.int32, (step_rows, 128), 1)
            turned = jnp.where(lanes == 0, peak, total).T[:8]
            part[r, pl.ds(first, owners)] = result
            for j in range(owners):
                stat[r, first + j] = turned[:, j * rows:(j + 1) * rows]
            for j in range(owners):
                owner = first + j

                @pl.when(owner != me)
                def _():
                    o_copy(r, owner, me).start()
                    s_copy(r, owner, me).start()

                @pl.when(owner == me)
                def _():
                    got[r, owner] = result[j]
                    got_stat[r, owner] = turned[:, j * rows:(j + 1) * rows]

        loop(0, steps, attend)

    for r in range(requests):
        def arrive(i, r=r):
            o_copy(r, me, other(i)).wait_recv()
            s_copy(r, me, other(i)).wait_recv()

        loop(1, n, arrive)

        def merge(k, r=r):
            stats = [got_stat[r, b * heads + k] for b in range(blocks)]
            top = functools.reduce(jnp.maximum, [s[0:1] for s in stats])
            shares = [s[1:2] * jnp.exp2(s[0:1] - top) for s in stats]
            whole = functools.reduce(jnp.add, shares)
            shares = jnp.concatenate([s / whole for s in shares], axis=0)
            fill = -blocks % 128
            shares = jnp.concatenate(
                [shares, jnp.zeros((fill, rows), jnp.float32)], axis=0).T
            merged = functools.reduce(jnp.add, [
                shares[:, b:b + 1] * got[r, b * heads + k].astype(jnp.float32)
                for b in range(blocks)])
            merged = merged.astype(jnp.bfloat16).reshape(local_rows, group, head_dim)
            out_ref[r, :, pl.ds(pl.multiple_of(k * group, group), group), :] = merged

        loop(0, heads, merge)

    loop(1, n, lambda i: q_copy(other(i), me).wait_send())
    loop(1, heads, lambda i: new_copy(peer(i), my_head).wait_send())
    for r in range(requests):
        def leave(i, r=r):
            k_copy(r, peer(i), my_head).wait_send()
            v_copy(r, peer(i), my_head).wait_send()

        loop(1, heads, leave)

        def leave_out(i, r=r):
            o_copy(r, other(i), me).wait_send()
            s_copy(r, other(i), me).wait_send()

        loop(1, n, leave_out)


def shards(queries, new_k, new_v, cache_k, cache_v, cache_len):
    requests, local_rows, q_heads, head_dim = queries.shape
    slots, heads = cache_k.shape[1:3]
    group = q_heads // heads
    n = lax.axis_size("seq")
    rows = local_rows * group
    padded = -(-local_rows // 16) * 16
    owners = max(w for w in range(1, n + 1) if n % w == 0 and w * rows <= max(256, rows))
    span = max(w for w in range(1, heads + 1) if heads % w == 0 and w * slots <= max(1024, slots))

    q = jnp.transpose(
        queries.reshape(requests, local_rows, heads, group, head_dim), (2, 0, 1, 3, 4)
    ).reshape(heads, requests, rows, head_dim)
    new = jnp.transpose(jnp.stack([new_k, new_v]), (3, 1, 0, 2, 4))
    new = jnp.pad(new, ((0, 0), (0, 0), (0, 0), (0, padded - local_rows), (0, 0)))
    k = jnp.transpose(cache_k, (2, 0, 1, 3))
    v = jnp.transpose(cache_v, (2, 0, 1, 3))

    bf16, f32, dma = jnp.bfloat16, jnp.float32, pltpu.SemaphoreType.DMA
    scratch = [
        pltpu.VMEM((requests, n, rows, head_dim), bf16),
        pltpu.VMEM((requests, 2, heads, padded, head_dim), bf16),
        pltpu.VMEM((requests, heads, slots, head_dim), bf16),
        pltpu.VMEM((requests, heads, slots, head_dim), bf16),
        pltpu.VMEM((requests, n, rows, head_dim), bf16),
        pltpu.VMEM((requests, n, 8, rows), f32),
        pltpu.VMEM((requests, n, rows, head_dim), bf16),
        pltpu.VMEM((requests, n, 8, rows), f32),
        dma((2 + 2 * requests,)),
        dma((n,)), dma((n,)), dma((heads,)), dma((heads,)),
        dma((requests, heads)), dma((requests, heads)),
        dma((requests, heads)), dma((requests, heads)),
        dma((requests, n)), dma((requests, n)), dma((requests, n)), dma((requests, n)),
    ]
    work = requests * n * rows * heads * slots
    vmem = pl.BlockSpec(memory_space=pltpu.VMEM)
    return pl.pallas_call(
        functools.partial(
            kernel, n, heads, requests, slots, local_rows, group, owners, span),
        out_shape=jax.ShapeDtypeStruct(queries.shape, bf16),
        in_specs=[pl.BlockSpec(memory_space=pltpu.SMEM)] + [vmem] * 4,
        out_specs=vmem,
        scratch_shapes=scratch,
        compiler_params=pltpu.CompilerParams(
            collective_id=0, has_side_effects=True, vmem_limit_bytes=52 * 1024 * 1024),
        cost_estimate=pl.CostEstimate(
            flops=4 * work * head_dim, bytes_accessed=4 * k.size, transcendentals=work),
    )(cache_len, q, new, k, v)


def solution(mesh):
    spec = P("groups", "seq", None, None)
    in_specs = (spec, spec, spec, spec, spec, P("groups"))
    return jax.shard_map(
        shards, mesh=mesh, in_specs=in_specs, out_specs=spec, check_vma=False)
```

time: 313 us -> 115 us (0.37)
  waiting for transfers between devices: 167 us -> 0 us
  Pallas kernels: 0 us -> 107 us
  starting transfers between devices: 44.9 us -> 0 us
  matrix products: 41 us -> 0 us
  other arithmetic: 31 us -> 0.02 us
  local copies, waits for them, and re-layouts: 25.7 us -> 7.82 us
    all_to_all x8 -> x0, waiting for transfers between devices: 167 us -> none  [the longest x1 44.3 us: shards(): lax.all_to_all(to_heads(cache_v), 'seq', split_axis=0, concat_axis=0, til...]
    pallas_call x0 -> x1, Pallas kernels: none -> 107 us  [shards(): pl.pallas_call(functools.partial(kernel, n, heads, requests, slots, local...]
    all_to_all x8 -> x0, starting transfers between devices: 44.9 us -> none  [the longest x1 6.58 us: shards(): lax.all_to_all(head_spread(new_v), 'seq', split_axis=0, concat_axis=1, ti...]
    dot_general x32 -> x0, matrix products: 41 us -> none  [the longest x8 19.3 us: head_block(): jnp.einsum('rpgsj,srjd->prgd', cache_weights, moved_v, preferred_element_...]
    reduce_sum x18 -> x0, other arithmetic: 22.5 us -> none  [the longest x16 21.7 us: head_block(): row_sum = jnp.sum(cache_weights, axis=-1) + jnp.sum(fresh_weights, axis=-1)]
    reshape x3 -> x1, local copies, waits for them, and re-layouts: 9.95 us -> 1.09 us  [shards(): queries.reshape(requests, local_rows, heads, group, head_dim)]
    unnamed x13 -> x3, local copies, waits for them, and re-layouts: 7.53 us -> 0.8 us
    lt x8 -> x0, other arithmetic: 5.97 us -> none  [shards(): head_valid = (slot_pos[None, :] < cache_len[:, None])[:, None, None, :]]
  transfers between devices with their start and end apart: 8 -> 0, of which waited for: 8 -> 0; matrix products, arithmetic and copies ran while one was open for 5% -> 0% of each run, Pallas kernels for 0% -> 0%
where the time goes in v1:
time: 115 us
  Pallas kernels  107 us (93%)
  local copies, waits for them, and re-layouts  7.82 us (7%)
    pallas_call x1, Pallas kernels, shards(): pl.pallas_call(functools.partial(kernel, n, heads, requests, slots, local...  107 us
    transpose x1, local copies, waits for them, and re-layouts, shards(): v = jnp.transpose(cache_v, (2, 0, 1, 3))  5.12 us

profile of v1, /device:TPU:9, one launch (start us, length us, event | category | flops | bytes accessed | tf_op | source)
XLA Modules:
  0.0 114.6 jit_solution(2311200818987132568)
XLA Ops:
  0.0 0.8 copy_bitcast_fusion.2
  0.8 1.1 copy.7
  1.9 0.0 copy-start
  1.9 5.1 %copy_bitcast_fusion = (bf16[8,2,512,128]{3,2,1,0:T(8,128)(2,1)}, bf16[8,2,512,128]{3,2,1,0:T(8,128)(2,1)}) fusion(bf16[2,512,8,128]{3,2,1,0:T(8,128)(2,1)} %param.10, bf16[2,512,8,128]{3,2,1,0:T(8,128)(2,1)} %param.9), kind=kLoop, calls=%fused_computation | loop fusion | bytes 8388608 | tf_op jit(solution)/shard_map/transpose | solution.py:228
  7.1 0.0 copy-done
  7.1 106.7 %shard_map.64 = bf16[2,8,128,128]{3,2,1,0:T(8,128)(2,1)S(1)} custom-call(s32[2]{0:T(128)S(1)} %copy-done, bf16[8,2,128,128]{3,2,1,0:T(8,128)(2,1)S(1)} %bitcast.14, bf16[8,2,2,16,128]{4,3,2,1,0:T(8,128)(2,1)S(1)} %pad.4.new_ref, bf16[8,2,512,128]{3,2,1,0:T(8,128)(2,1)} %get-tuple-element.8.k_ref, bf16[8,2,512,128]{3,2,1,0:T(8,128)(2,1)} %get-tuple-element.7.v_ref), custom_call_target="tpu_custom_call" | custom-call | flops 8589934592 | bytes 4194304 | tf_op jit(solution)/shard_map/pallas_call | solution.py:248
  113.8 0.8 copy.17
  (2 shorter events, 0.0 us)
Async XLA Ops:
  1.9 5.1 %copy-start = (s32[2]{0:T(128)S(1)}, s32[2]{0:T(128)}, u32[]{:S(2)}) copy-start(s32[2]{0:T(128)} %len_ref.1) | copy-start | bytes 28

commit v2 on v1

--- a/solution.py
+++ b/solution.py
@@ -148,7 +148,7 @@
             peak, total, value = absorb(
                 state, jnp.where(valid, score(keys), LOW), values)
 
-            result = (value / total).astype(jnp.bfloat16).reshape(owners, rows, head_dim)
+            result = (value * (1.0 / total)).astype(jnp.bfloat16).reshape(owners, rows, head_dim)
             lanes = lax.broadcasted_iota(jnp.int32, (step_rows, 128), 1)
             turned = jnp.where(lanes == 0, peak, total).T[:8]
             part[r, pl.ds(first, owners)] = result
@@ -176,22 +176,22 @@
 
         loop(1, n, arrive)
 
-        def merge(k, r=r):
-            stats = [got_stat[r, b * heads + k] for b in range(blocks)]
-            top = functools.reduce(jnp.maximum, [s[0:1] for s in stats])
-            shares = [s[1:2] * jnp.exp2(s[0:1] - top) for s in stats]
-            whole = functools.reduce(jnp.add, shares)
-            shares = jnp.concatenate([s / whole for s in shares], axis=0)
-            fill = -blocks % 128
-            shares = jnp.concatenate(
-                [shares, jnp.zeros((fill, rows), jnp.float32)], axis=0).T
+        stats = [got_stat[r, b * heads:(b + 1) * heads] for b in range(blocks)]
+        top = functools.reduce(jnp.maximum, [s[:, 0] for s in stats])
+        shares = [s[:, 1] * jnp.exp2(s[:, 0] - top) for s in stats]
+        whole = functools.reduce(jnp.add, shares)
+        shares = [s / whole for s in shares]
+        fill = -n % 128
+        if fill:
+            shares.append(jnp.zeros((fill, rows), jnp.float32))
+        shares = jnp.concatenate(shares, axis=0).T
+        for k in range(heads):
             merged = functools.reduce(jnp.add, [
-                shares[:, b:b + 1] * got[r, b * heads + k].astype(jnp.float32)
+                shares[:, b * heads + k:b * heads + k + 1]
+                * got[r, b * heads + k].astype(jnp.float32)
                 for b in range(blocks)])
             merged = merged.astype(jnp.bfloat16).reshape(local_rows, group, head_dim)
-            out_ref[r, :, pl.ds(pl.multiple_of(k * group, group), group), :] = merged
-
-        loop(0, heads, merge)
+            out_ref[r, :, k * group:(k + 1) * group, :] = merged
 
     loop(1, n, lambda i: q_copy(other(i), me).wait_send())
     loop(1, heads, lambda i: new_copy(peer(i), my_head).wait_send())
@@ -216,7 +216,7 @@
     n = lax.axis_size("seq")
     rows = local_rows * group
     padded = -(-local_rows // 16) * 16
-    owners = max(w for w in range(1, n + 1) if n % w == 0 and w * rows <= max(256, rows))
+    owners = max(w for w in range(1, n + 1) if n % w == 0 and w * rows <= max(512, rows))
     span = max(w for w in range(1, heads + 1) if heads % w == 0 and w * slots <= max(1024, slots))
 
     q = jnp.transpose(

time: 115 us -> 107 us (0.930)
  Pallas kernels: 107 us -> 97.8 us
    pallas_call x1, Pallas kernels: 107 us -> 97.8 us  [shards(): pl.pallas_call(functools.partial(kernel, n, heads, requests, slots, local...]
where the time goes in v2:
time: 107 us; the launch traced here: 106 us
  Pallas kernels  97.8 us (91%)
  local copies, waits for them, and re-layouts  7.82 us (7%)
    pallas_call x1, Pallas kernels, shards(): pl.pallas_call(functools.partial(kernel, n, heads, requests, slots, local...  97.8 us
    transpose x1, local copies, waits for them, and re-layouts, shards(): v = jnp.transpose(cache_v, (2, 0, 1, 3))  5.12 us

profile of v2, /device:TPU:9, one launch (start us, length us, event | category | flops | bytes accessed | tf_op | source)
XLA Modules:
  0.0 105.7 jit_solution(14083558630365120286)
XLA Ops:
  0.0 0.8 copy_bitcast_fusion.2
  0.8 1.1 %copy.7 = bf16[2,8,8,16,128]{4,3,1,0,2:T(8,128)(2,1)S(1)} copy(bf16[2,8,8,16,128]{4,3,2,1,0:T(8,128)(2,1)} %bitcast.15) | data formatting | bytes 1048576 | tf_op jit(solution)/shard_map/reshape | solution.py:223
  1.9 0.0 copy-start
  1.9 5.1 %copy_bitcast_fusion = (bf16[8,2,512,128]{3,2,1,0:T(8,128)(2,1)}, bf16[8,2,512,128]{3,2,1,0:T(8,128)(2,1)}) fusion(bf16[2,512,8,128]{3,2,1,0:T(8,128)(2,1)} %param.10, bf16[2,512,8,128]{3,2,1,0:T(8,128)(2,1)} %param.9), kind=kLoop, calls=%fused_computation | loop fusion | bytes 8388608 | tf_op jit(solution)/shard_map/transpose | solution.py:228
  7.1 0.0 copy-done
  7.1 97.8 %shard_map.64 = bf16[2,8,128,128]{3,2,1,0:T(8,128)(2,1)S(1)} custom-call(s32[2]{0:T(128)S(1)} %copy-done, bf16[8,2,128,128]{3,2,1,0:T(8,128)(2,1)S(1)} %bitcast.14, bf16[8,2,2,16,128]{4,3,2,1,0:T(8,128)(2,1)S(1)} %pad.4.new_ref, bf16[8,2,512,128]{3,2,1,0:T(8,128)(2,1)} %get-tuple-element.8.k_ref, bf16[8,2,512,128]{3,2,1,0:T(8,128)(2,1)} %get-tuple-element.7.v_ref), custom_call_target="tpu_custom_call" | custom-call | flops 8589934592 | bytes 4194304 | tf_op jit(solution)/shard_map/pallas_call | solution.py:248
  104.9 0.8 copy.17
  (2 shorter events, 0.0 us)
Async XLA Ops:
  1.9 5.1 %copy-start = (s32[2]{0:T(128)S(1)}, s32[2]{0:T(128)}, u32[]{:S(2)}) copy-start(s32[2]{0:T(128)} %len_ref.1) | copy-start | bytes 28

commit v3 on v2

--- a/solution.py
+++ b/solution.py
@@ -22,7 +22,7 @@
 
 def kernel(
     n, heads, requests, slots, local_rows, group, owners, span,
-    len_ref, q_ref, new_ref, k_ref, v_ref, out_ref,
+    len_ref, q_ref, new_ref, cache_k_ref, cache_v_ref, out_ref, k_ref, v_ref, wide,
     all_q, all_new, all_k, all_v, part, stat, got, got_stat,
     own_sem, q_send, q_recv, new_send, new_recv, k_send, k_recv, v_send, v_recv,
     o_send, o_recv, s_send, s_recv,
@@ -76,8 +76,15 @@
 
     loop(1, n, lambda i: q_copy(other(i), me).start())
     loop(1, heads, lambda i: new_copy(peer(i), my_head).start())
-    for r in range(requests):
+    def turn(cache_ref, turned_ref, r):
+        wide[...] = cache_ref[r].astype(jnp.float32).reshape(slots * heads, head_dim)
+        for h in range(heads):
+            turned_ref[h, r] = wide[pl.ds(h, slots, stride=heads), :].astype(jnp.bfloat16)
+
+    for r in range(requests):
+        turn(cache_k_ref, k_ref, r)
         loop(1, heads, lambda i: k_copy(r, peer(i), my_head).start())
+        turn(cache_v_ref, v_ref, r)
         loop(1, heads, lambda i: v_copy(r, peer(i), my_head).start())
 
     own = [
@@ -224,11 +231,12 @@
     ).reshape(heads, requests, rows, head_dim)
     new = jnp.transpose(jnp.stack([new_k, new_v]), (3, 1, 0, 2, 4))
     new = jnp.pad(new, ((0, 0), (0, 0), (0, 0), (0, padded - local_rows), (0, 0)))
-    k = jnp.transpose(cache_k, (2, 0, 1, 3))
-    v = jnp.transpose(cache_v, (2, 0, 1, 3))
 
     bf16, f32, dma = jnp.bfloat16, jnp.float32, pltpu.SemaphoreType.DMA
     scratch = [
+        pltpu.VMEM((heads, requests, slots, head_dim), bf16),
+        pltpu.VMEM((heads, requests, slots, head_dim), bf16),
+        pltpu.VMEM((slots * heads, head_dim), f32),
         pltpu.VMEM((requests, n, rows, head_dim), bf16),
         pltpu.VMEM((requests, 2, heads, padded, head_dim), bf16),
         pltpu.VMEM((requests, heads, slots, head_dim), bf16),
@@ -255,8 +263,8 @@
         compiler_params=pltpu.CompilerParams(
             collective_id=0, has_side_effects=True, vmem_limit_bytes=52 * 1024 * 1024),
         cost_estimate=pl.CostEstimate(
-            flops=4 * work * head_dim, bytes_accessed=4 * k.size, transcendentals=work),
-    )(cache_len, q, new, k, v)
+            flops=4 * work * head_dim, bytes_accessed=4 * cache_k.size, transcendentals=work),
+    )(cache_len, q, new, cache_k, cache_v)
 
 
 def solution(mesh):

time: 107 us -> 103 us (0.963)
  local copies, waits for them, and re-layouts: 7.82 us -> 3.34 us
    transpose x1 -> x0, local copies, waits for them, and re-layouts: 5.12 us -> none  [shards(): v = jnp.transpose(cache_v, (2, 0, 1, 3))]
where the time goes in v3:
time: 103 us; the launch traced here: 101 us
  Pallas kernels  97.8 us (95%)
  local copies, waits for them, and re-layouts  3.34 us (3%)
    pallas_call x1, Pallas kernels, shards(): pl.pallas_call(functools.partial(kernel, n, heads, requests, slots, local...  97.8 us

profile of v3, /device:TPU:9, one launch (start us, length us, event | category | flops | bytes accessed | tf_op | source)
XLA Modules:
  0.0 101.2 jit_solution(11598208418948503221)
XLA Ops:
  0.0 0.8 copy_bitcast_fusion
  0.8 1.1 %copy.7 = bf16[2,8,8,16,128]{4,3,1,0,2:T(8,128)(2,1)S(1)} copy(bf16[2,8,8,16,128]{4,3,2,1,0:T(8,128)(2,1)} %bitcast.11) | data formatting | bytes 1048576 | tf_op jit(solution)/shard_map/reshape | solution.py:230
  1.9 0.0 copy-start
  1.9 0.6 copy-done
  2.6 97.8 %shard_map.64 = bf16[2,8,128,128]{3,2,1,0:T(8,128)(2,1)S(1)} custom-call(s32[2]{0:T(128)S(1)} %copy-done, bf16[8,2,128,128]{3,2,1,0:T(8,128)(2,1)S(1)} %bitcast.10, bf16[8,2,2,16,128]{4,3,2,1,0:T(8,128)(2,1)S(1)} %pad.4.new_ref, bf16[2,512,8,128]{3,2,1,0:T(8,128)(2,1)} %cache_k_ref.1, bf16[2,512,8,128]{3,2,1,0:T(8,128)(2,1)} %cache_v_ref.1), custom_call_target="tpu_custom_call" | custom-call | flops 8589934592 | bytes 4194304 | tf_op jit(solution)/shard_map/pallas_call | solution.py:256
  100.4 0.8 copy.13
  (2 shorter events, 0.0 us)
Async XLA Ops:
  1.9 0.7 copy-start

commit v4 on v3

--- a/solution.py
+++ b/solution.py
@@ -37,9 +37,15 @@
     head_dim = q_ref.shape[-1]
     factor = math.log2(math.e) / math.sqrt(head_dim)
 
+    def turn(cache_ref, turned_ref, r):
+        wide[...] = cache_ref[r].astype(jnp.float32).reshape(slots * heads, head_dim)
+        for h in range(heads):
+            turned_ref[h, r] = wide[pl.ds(h, slots, stride=heads), :].astype(jnp.bfloat16)
+
     barrier = pltpu.get_barrier_semaphore()
     loop(1, n, lambda i: pl.semaphore_signal(
         barrier, inc=1, device_id={"seq": lax.rem(me + i, n)}, device_id_type=MESH))
+    turn(cache_k_ref, k_ref, 0)
     pl.semaphore_wait(barrier, n - 1)
 
     def remote(src, dst, send, recv, device):
@@ -76,13 +82,9 @@
 
     loop(1, n, lambda i: q_copy(other(i), me).start())
     loop(1, heads, lambda i: new_copy(peer(i), my_head).start())
-    def turn(cache_ref, turned_ref, r):
-        wide[...] = cache_ref[r].astype(jnp.float32).reshape(slots * heads, head_dim)
-        for h in range(heads):
-            turned_ref[h, r] = wide[pl.ds(h, slots, stride=heads), :].astype(jnp.bfloat16)
-
-    for r in range(requests):
-        turn(cache_k_ref, k_ref, r)
+    for r in range(requests):
+        if r > 0:
+            turn(cache_k_ref, k_ref, r)
         loop(1, heads, lambda i: k_copy(r, peer(i), my_head).start())
         turn(cache_v_ref, v_ref, r)
         loop(1, heads, lambda i: v_copy(r, peer(i), my_head).start())

time: 103 us -> 103 us (level)
  no operation moved by 1% of the time
where the time goes in v4:
time: 103 us; the launch traced here: 101 us
  Pallas kernels  97.8 us (95%)
  local copies, waits for them, and re-layouts  3.34 us (3%)
    pallas_call x1, Pallas kernels, shards(): pl.pallas_call(functools.partial(kernel, n, heads, requests, slots, local...  97.8 us

profile of v4, /device:TPU:9, one launch (start us, length us, event | category | flops | bytes accessed | tf_op | source)
XLA Modules:
  0.0 101.2 jit_solution(17596038935143790972)
XLA Ops:
  0.0 0.8 copy_bitcast_fusion
  0.8 1.1 %copy.7 = bf16[2,8,8,16,128]{4,3,1,0,2:T(8,128)(2,1)S(1)} copy(bf16[2,8,8,16,128]{4,3,2,1,0:T(8,128)(2,1)} %bitcast.11) | data formatting | bytes 1048576 | tf_op jit(solution)/shard_map/reshape | solution.py:232
  1.9 0.0 copy-start
  1.9 0.6 copy-done
  2.6 97.8 %shard_map.64 = bf16[2,8,128,128]{3,2,1,0:T(8,128)(2,1)S(1)} custom-call(s32[2]{0:T(128)S(1)} %copy-done, bf16[8,2,128,128]{3,2,1,0:T(8,128)(2,1)S(1)} %bitcast.10, bf16[8,2,2,16,128]{4,3,2,1,0:T(8,128)(2,1)S(1)} %pad.4.new_ref, bf16[2,512,8,128]{3,2,1,0:T(8,128)(2,1)} %cache_k_ref.1, bf16[2,512,8,128]{3,2,1,0:T(8,128)(2,1)} %cache_v_ref.1), custom_call_target="tpu_custom_call" | custom-call | flops 8589934592 | bytes 4194304 | tf_op jit(solution)/shard_map/pallas_call | solution.py:258
  100.4 0.8 copy.13
  (2 shorter events, 0.0 us)
Async XLA Ops:
  1.9 0.7 copy-start
